TPU v7x, 256 devices: a whole 4x4x8 slice. The times are simulated.
256 devices in a mesh: seq: 8 (over x, core), head: 32 (over y, z).
Axes of the slice: x: 4, y: 4, z: 8, core: 2. Of those that a mesh axis runs over, the one named last changes fastest.
Arguments:
- inputs: bfloat16 [81920, 8192], P(('seq', 'head')), may hold values from -6 to 6
- b_panel: bfloat16 [81920, 128], P(('seq', 'head')), may hold values from -0.52734375 to 0.52734375
- c_panel: bfloat16 [81920, 128], P(('seq', 'head')), may hold values from -0.52734375 to 0.52734375
- dt_raw: bfloat16 [81920, 128], P(('seq', 'head')), may hold values from -3 to 3
- dt_bias: float32 [128], replicated, may hold values from -3.5 to 0.5
- a_log: float32 [128], replicated, may hold values from -12 to 1
- d_skip: float32 [128], replicated, may hold values from 0.5 to 1.5
Outputs:
- mixed: bfloat16 [81920, 8192], P(('seq', 'head'))
All inputs are finite; a program needn't handle non-finite values.
Results may differ from a plain program's by a relative error of at most 0.0051.
Values may be sent and summed in bfloat16 or wider, within the bound.
A program may use at most 128 MiB of HBM per device.

v0:
```python
import jax
import jax.numpy as jnp
from jax import lax
from jax.sharding import PartitionSpec as P

HEADS = 128
HDIM = 64
DSTATE = 128
SPAN = 256


def passed_along(block, axis, distance):
    devices = range(lax.axis_size(axis))
    route = [(i - distance, i) for i in devices if i - distance in devices]
    return lax.ppermute(block, axis, route)


def head_terms(cumulative, delta_head, tokens_head, scores, b_spans):
    positions = jnp.arange(SPAN, dtype=jnp.int32)
    causal_mask = positions[:, None] >= positions[None, :]
    spread = cumulative[:, :, None] - cumulative[:, None, :]
    decays = jnp.exp(jnp.where(causal_mask[None], spread, -1e30))
    weights = (scores * decays * delta_head[:, None, :]).astype(jnp.bfloat16)
    within = jnp.einsum("kts,ksp->ktp", weights, tokens_head, preferred_element_type=jnp.float32)
    ending = cumulative[:, -1:]
    scaled_b = (b_spans * (jnp.exp(ending - cumulative) * delta_head)[:, :, None]).astype(
        jnp.bfloat16
    )
    span_state = jnp.einsum(
        "ksn,ksp->knp", scaled_b, tokens_head, preferred_element_type=jnp.float32
    )
    return (within, span_state, jnp.exp(ending[:, 0]))


def on_device(inputs, b_panel, c_panel, dt_raw, dt_bias, a_log, d_skip):
    groups = lax.axis_size("head")
    local_heads = HEADS // groups
    tokens, raw_steps = (
        lax.all_to_all(inputs, "head", split_axis=1, concat_axis=0, tiled=True),
        lax.all_to_all(dt_raw, "head", split_axis=1, concat_axis=0, tiled=True),
    )
    b_whole, c_whole = (
        lax.all_gather(b_panel, "head", axis=0, tiled=True),
        lax.all_gather(c_panel, "head", axis=0, tiled=True),
    )
    length = tokens.shape[0]
    blocks = length // SPAN
    first_head = lax.axis_index("head") * local_heads
    bias_here = lax.dynamic_slice_in_dim(dt_bias, first_head, local_heads)
    alog_here = lax.dynamic_slice_in_dim(a_log, first_head, local_heads)
    skip_here = lax.dynamic_slice_in_dim(d_skip, first_head, local_heads)
    delta = jax.nn.softplus(raw_steps.astype(jnp.float32) + bias_here[None, :])
    rates = -jnp.exp(alog_here)[None, :] * delta
    cumulative = jnp.cumsum(rates.reshape(blocks, SPAN, local_heads), axis=1)
    delta_blocks = delta.reshape(blocks, SPAN, local_heads)
    b_spans = b_whole.reshape(blocks, SPAN, DSTATE)
    c_spans = c_whole.reshape(blocks, SPAN, DSTATE)
    scores = jnp.einsum("ktn,ksn->kts", c_spans, b_spans, preferred_element_type=jnp.float32)
    tokens_all = tokens.reshape(blocks, SPAN, local_heads, HDIM)

    def one_head(head):
        tokens_head = lax.dynamic_index_in_dim(tokens_all, head, 2, keepdims=False)
        cum_head = lax.dynamic_index_in_dim(cumulative, head, 2, keepdims=False)
        delta_head = lax.dynamic_index_in_dim(delta_blocks, head, 2, keepdims=False)
        return head_terms(cum_head, delta_head, tokens_head, scores, b_spans)

    within, span_state, span_decay = lax.map(one_head, jnp.arange(local_heads, dtype=jnp.int32))

    def advance(running, pieces):
        state_now, product = running
        factor, update = pieces
        return (
            (factor[:, None, None] * state_now + update, product * factor),
            (state_now, product),
        )

    start_state = (
        jnp.zeros((local_heads, DSTATE, HDIM), jnp.float32),
        jnp.ones((local_heads,), jnp.float32),
    )
    finals, befores = lax.scan(
        advance, start_state, (jnp.transpose(span_decay), jnp.moveaxis(span_state, 1, 0))
    )
    final_state, total_decay = finals
    entering, prefix_decay = befores
    incoming = jnp.zeros((local_heads, DSTATE, HDIM), jnp.float32)
    for turn_index in range(lax.axis_size("seq") - 1):
        leaving = total_decay[:, None, None] * incoming + final_state
        incoming = passed_along(leaving, "seq", 1)
    states = entering + prefix_decay[:, :, None, None] * incoming[None]
    states_b = states.astype(jnp.bfloat16)
    carried = jnp.einsum("ktn,khnp->kthp", c_spans, states_b, preferred_element_type=jnp.float32)
    ordered = jnp.transpose(within, (1, 2, 0, 3))
    combined = (
        ordered
        + carried * jnp.exp(cumulative)[..., None]
        + skip_here[:, None] * tokens_all.astype(jnp.float32)
    )
    result = combined.astype(jnp.bfloat16).reshape(length, local_heads * HDIM)
    return lax.all_to_all(result, "head", split_axis=0, concat_axis=1, tiled=True)


def solution(mesh):
    return jax.shard_map(
        on_device,
        mesh=mesh,
        in_specs=(
            P(("seq", "head"), None),
            P(("seq", "head"), None),
            P(("seq", "head"), None),
            P(("seq", "head"), None),
            P(),
            P(),
            P(),
        ),
        out_specs=P(("seq", "head"), None),
        check_vma=False,
    )
```

profile of v0, /device:TPU:2, one launch (start us, length us, event | category | flops | bytes accessed | tf_op | source)
XLA Modules:
  0.0 611.0 jit_solution(6843153276479366639)
XLA Ops:
  8.9 11.5 %all-to-all-start = ((bf16[320,32,4]{0,2,1:T(4,128)(2,1)}), bf16[320,32,4]{0,2,1:T(4,128)(2,1)S(1)}, u32[]{:S(2)}, u32[]{:S(2)}) async-start(bf16[320,32,4]{0,2,1:T(4,128)(2,1)} %all_to_all.36), calls=%async_computation | async-start | bytes 196608 | tf_op jit(solution)/shard_map/all_to_all | solution.py:40
  20.4 5.4 copy.114
  25.9 4.7 all-to-all-done
  30.6 5.3 all-to-all-start.1
  37.3 2.4 reduce-window.6
  40.0 75.6 %all-gather.3.cloned.1.call-done = bf16[10240,128]{1,0:T(8,128)(2,1)} async-done(((bf16[320,128]{1,0:T(8,128)(2,1)}), bf16[10240,128]{1,0:T(8,128)(2,1)}) %all-gather.3.cloned.1.call-update) | async-done | bytes 2621456 | tf_op jit(solution)/shard_map/all_gather | solution.py:44
  115.6 93.1 %all-gather.5.cloned.1.call-done = bf16[10240,128]{1,0:T(8,128)(2,1)} async-done(((bf16[320,128]{1,0:T(8,128)(2,1)}), bf16[10240,128]{1,0:T(8,128)(2,1)}) %all-gather.5.cloned.1.call-update) | async-done | bytes 2621456 | tf_op jit(solution)/shard_map/all_gather | solution.py:43
  208.8 7.9 %fusion.19 = f32[40,256,256]{2,1,0:T(8,128)} fusion(bf16[40,256,128]{2,1,0:T(8,128)(2,1)} %bitcast.108, bf16[40,256,128]{2,1,0:T(8,128)(2,1)} %bitcast.111), kind=kOutput, calls=%fused_computation.52 | convolution fusion | flops 671088640 | bytes 15728640 | tf_op jit(solution)/shard_map/ktn,ksn->kts/dot_general | solution.py:58
  216.6 8.7 %copy.81 = bf16[32,320,256]{1,0,2:T(8,128)(2,1)} copy(bf16[32,320,256]{2,1,0:T(8,128)(2,1)} %bitcast.12) | data formatting | bytes 10485760 | tf_op jit(solution)/shard_map/all_to_all | solution.py:39
  225.3 13.2 %reshape.98 = bf16[40,256,4,64]{1,0,3,2:T(8,128)(2,1)} reshape(bf16[32,320,256]{1,0,2:T(8,128)(2,1)} %copy.81) | data formatting | bytes 10485760 | tf_op jit(solution)/shard_map/reshape | solution.py:59
  238.5 56.5 %while.31 = (s32[]{:T(128)}, f32[4,40,256,64]{2,3,0,1:T(8,128)}, f32[4,40,128,64]{2,3,1,0:T(8,128)}, f32[4,40]{1,0:T(4,128)S(1)}, s32[4]{0:T(128)S(1)}, /*index=...) while((s32[]{:T(128)}, f32[4,40,256,64]{2,3,0,1:T(8,128)}, ...), condition=%wide.region_3.4_spmd, body=%wide.region_2.3_spmd.sunk | while | flops 520441856 | bytes 22825084 | solution.py:67
  241.1 1.4 constant_dynamic-slice_fusion.3
  242.6 6.8 %bitcast_dynamic-update-slice_fusion.4 = f32[4,40,256,64]{2,3,0,1:T(8,128)} fusion(f32[4,40,256,64]{2,3,0,1:T(8,128)} %get-tuple-element.365, s32[]{:T(128)} %get-tuple-element.364, f32[40,256,256]{2,1,0:T(8,128)} %get-tuple-element.383, f32[40,256]{1,0:T(8,128)S(1)} %get-tuple-element.338, f32[40,256]{1,0:T(8,128)S(1)} %dynamic-slice_bitcast_fusion.3, ...), kind=kOutput, calls=%fused_computation.12.clone.1 | convolution fusion | flops 348651520 | bytes 14606848 | tf_op jit(solution)/shard_map/while/body/eval_jaxpr/kts,ksp->ktp/dot_general | solution.py:24
  249.4 3.2 fusion.26
  255.2 1.4 constant_dynamic-slice_fusion.3
  256.7 6.8 %bitcast_dynamic-update-slice_fusion.4 = f32[4,40,256,64]{2,3,0,1:T(8,128)} fusion(f32[4,40,256,64]{2,3,0,1:T(8,128)} %get-tuple-element.365, s32[]{:T(128)} %get-tuple-element.364, f32[40,256,256]{2,1,0:T(8,128)} %get-tuple-element.383, f32[40,256]{1,0:T(8,128)S(1)} %get-tuple-element.338, f32[40,256]{1,0:T(8,128)S(1)} %dynamic-slice_bitcast_fusion.3, ...), kind=kOutput, calls=%fused_computation.12.clone.1 | convolution fusion | flops 348651520 | bytes 14606848 | tf_op jit(solution)/shard_map/while/body/eval_jaxpr/kts,ksp->ktp/dot_general | solution.py:24
  263.5 3.2 fusion.26
  269.3 1.4 constant_dynamic-slice_fusion.3
  270.8 6.9 %bitcast_dynamic-update-slice_fusion.4 = f32[4,40,256,64]{2,3,0,1:T(8,128)} fusion(f32[4,40,256,64]{2,3,0,1:T(8,128)} %get-tuple-element.365, s32[]{:T(128)} %get-tuple-element.364, f32[40,256,256]{2,1,0:T(8,128)} %get-tuple-element.383, f32[40,256]{1,0:T(8,128)S(1)} %get-tuple-element.338, f32[40,256]{1,0:T(8,128)S(1)} %dynamic-slice_bitcast_fusion.3, ...), kind=kOutput, calls=%fused_computation.12.clone.1 | convolution fusion | flops 348651520 | bytes 14606848 | tf_op jit(solution)/shard_map/while/body/eval_jaxpr/kts,ksp->ktp/dot_general | solution.py:24
  277.6 3.2 fusion.26
  283.5 1.4 constant_dynamic-slice_fusion.3
  284.9 6.8 %bitcast_dynamic-update-slice_fusion.4 = f32[4,40,256,64]{2,3,0,1:T(8,128)} fusion(f32[4,40,256,64]{2,3,0,1:T(8,128)} %get-tuple-element.365, s32[]{:T(128)} %get-tuple-element.364, f32[40,256,256]{2,1,0:T(8,128)} %get-tuple-element.383, f32[40,256]{1,0:T(8,128)S(1)} %get-tuple-element.338, f32[40,256]{1,0:T(8,128)S(1)} %dynamic-slice_bitcast_fusion.3, ...), kind=kOutput, calls=%fused_computation.12.clone.1 | convolution fusion | flops 348651520 | bytes 14606848 | tf_op jit(solution)/shard_map/while/body/eval_jaxpr/kts,ksp->ktp/dot_general | solution.py:24
  291.7 3.2 fusion.26
  295.0 8.5 %copy.85 = f32[4,40,128,64]{3,2,0,1:T(8,128)} copy(f32[4,40,128,64]{2,3,1,0:T(8,128)} %get-tuple-element.101) | data formatting | bytes 10485760 | tf_op jit(solution)/shard_map/while | solution.py:67
  303.5 74.1 %while.32 = (s32[]{:T(128)}, f32[4,128,64]{2,1,0:T(8,128)S(1)}, f32[4]{0:T(128)S(1)}, f32[40,4,128,64]{3,2,1,0:T(8,128)}, f32[40,4]{1,0:T(8,128)S(1)}, /*index=5...) while((s32[]{:T(128)}, f32[4,128,64]{2,1,0:T(8,128)S(1)}, ...), condition=%wide.region_5.6_spmd.clone, body=%wide.region_4.5_spmd.clone.sunk | while | flops 131083 | bytes 787189 | solution.py:81
  304.3 1.2 bitcast_add_fusion.2
  306.3 1.0 bitcast_add_fusion.2
  308.1 1.0 bitcast_add_fusion.2
  309.9 1.0 bitcast_add_fusion.2
  313.6 1.0 bitcast_add_fusion.2
  317.4 1.0 bitcast_add_fusion.2
  319.2 1.0 bitcast_add_fusion.2
  324.7 1.0 bitcast_add_fusion.2
  328.4 1.0 bitcast_add_fusion.2
  330.3 1.0 bitcast_add_fusion.2
  332.1 1.0 bitcast_add_fusion.2
  334.0 1.0 bitcast_add_fusion.2
  335.8 1.0 bitcast_add_fusion.2
  337.7 1.0 bitcast_add_fusion.2
  339.5 1.0 bitcast_add_fusion.2
  341.4 1.0 bitcast_add_fusion.2
  346.9 1.0 bitcast_add_fusion.2
  352.5 1.0 bitcast_add_fusion.2
  354.3 1.0 bitcast_add_fusion.2
  356.1 1.0 bitcast_add_fusion.2
  377.7 1.9 collective-permute-start
  379.7 5.8 collective-permute-done
  385.5 1.9 collective-permute-start.1
  387.4 5.8 collective-permute-done.1
  393.3 1.9 collective-permute-start.2
  395.2 5.8 collective-permute-done.2
  401.1 1.9 collective-permute-start.3
  403.0 5.8 collective-permute-done.3
  408.9 1.9 collective-permute-start.4
  410.8 5.8 collective-permute-done.4
  416.7 1.9 collective-permute-start.5
  418.7 5.7 collective-permute-done.5
  424.5 2.1 collective-permute-start.6
  426.8 5.4 collective-permute-done.6
  432.1 14.5 %fusion.12 = bf16[40,256,4,64]{1,3,2,0:T(8,128)(2,1)} fusion(f32[4,40,256,64]{2,3,0,1:T(8,128)} %get-tuple-element.99, bf16[40,256,4,64]{1,0,3,2:T(8,128)(2,1)} %get-tuple-element.419, f32[4]{0:T(128)S(1)} %dynamic_slice.34, f32[40,256,4]{1,2,0:T(4,128)S(1)} %copy.87, bf16[40,256,128,1]{2,1,3,0:T(8,128)(2,1)S(1)} %bitcast.109, ...), kind=kOutput, calls=%fused_computation.28 | convolution fusion | flops 690749440 | bytes 29131408 | tf_op jit(solution)/shard_map/ktn,khnp->kthp/dot_general | solution.py:92
  446.6 15.3 %copy.94 = bf16[40,256,4,64]{3,2,1,0:T(4,128)(2,1)} copy(bf16[40,256,4,64]{1,3,2,0:T(8,128)(2,1)} %fusion.12) | data formatting | bytes 10485760 | tf_op jit(solution)/shard_map/all_to_all | solution.py:100
  462.0 15.7 %reshape.101 = bf16[32,320,256]{2,1,0:T(8,128)(2,1)} reshape(bf16[40,256,4,64]{3,2,1,0:T(4,128)(2,1)} %copy.94) | data formatting | bytes 10485760 | tf_op jit(solution)/shard_map/all_to_all | solution.py:100
  477.7 123.5 %all_to_all.48 = bf16[32,320,256]{2,1,0:T(8,128)(2,1)S(1)} all-to-all(bf16[32,320,256]{2,1,0:T(8,128)(2,1)} %reshape.101), channel_id=1, replica_groups=mesh['seq'=8,'head'=32] {'head'}, dimensions={0} | all-to-all | bytes 10485760 | tf_op jit(solution)/shard_map/all_to_all | solution.py:100
  601.2 3.0 copy.104
  (212 shorter events, 61.0 us)
Async XLA Ops:
  6.5 109.1 %all-gather.3.cloned.1.call-start = ((), (), s32[]{:S(2)}) async-start(), calls=%async_computation.3 | async-start | bytes 2703360 | tf_op jit(solution)/shard_map/all_gather | solution.py:44
  8.9 21.6 %all-to-all-start = ((bf16[320,32,4]{0,2,1:T(4,128)(2,1)}), bf16[320,32,4]{0,2,1:T(4,128)(2,1)S(1)}, u32[]{:S(2)}, u32[]{:S(2)}) async-start(bf16[320,32,4]{0,2,1:T(4,128)(2,1)} %all_to_all.36), calls=%async_computation | async-start | bytes 196608 | tf_op jit(solution)/shard_map/all_to_all | solution.py:40
  30.6 6.2 %copy-start.2 = (f32[128]{0:T(128)S(1)}, f32[128]{0:T(128)}, u32[]{:S(2)}) copy-start(f32[128]{0:T(128)} %param.15) | copy-start | bytes 1540
  30.6 6.2 %copy-start.3 = (f32[128]{0:T(128)S(1)}, f32[128]{0:T(128)}, u32[]{:S(2)}) copy-start(f32[128]{0:T(128)} %param.16) | copy-start | bytes 1540
  30.6 186.1 %all-to-all-start.1 = ((bf16[320,32,256]{2,0,1:T(8,128)(2,1)}), bf16[320,32,256]{2,0,1:T(8,128)(2,1)}, u32[]{:S(2)}, u32[]{:S(2)}) async-start(bf16[320,32,256]{2,0,1:T(8,128)(2,1)} %bitcast.105), calls=%async_computation.1 | async-start | bytes 10485760 | tf_op jit(solution)/shard_map/all_to_all | solution.py:39
  35.9 172.8 %all-gather.5.cloned.1.call-start = ((), (), s32[]{:S(2)}) async-start(), calls=%async_computation.4 | async-start | bytes 2703360 | tf_op jit(solution)/shard_map/all_gather | solution.py:43
  225.3 13.2 %copy-start.1 = (bf16[10240,128]{1,0:T(8,128)(2,1)S(1)}, bf16[10240,128]{1,0:T(8,128)(2,1)}, u32[]{:S(2)}) copy-start(bf16[10240,128]{1,0:T(8,128)(2,1)} %all-gather.5.cloned.1.call-done) | copy-start | bytes 7864324
  303.5 115.1 %copy-start.4 = (f32[128]{0:T(128)S(1)}, f32[128]{0:T(128)}, u32[]{:S(2)}) copy-start(f32[128]{0:T(128)} %param.17) | copy-start | bytes 1540
  303.5 128.6 %copy-start = (bf16[10240,128]{1,0:T(8,128)(2,1)S(1)}, bf16[10240,128]{1,0:T(8,128)(2,1)}, u32[]{:S(2)}) copy-start(bf16[10240,128]{1,0:T(8,128)(2,1)} %all-gather.3.cloned.1.call-done) | copy-start | bytes 7864324
  377.7 7.7 %collective-permute-start = (f32[4,128,64]{2,1,0:T(8,128)S(1)}, f32[4,128,64]{2,1,0:T(8,128)S(1)}, u32[]{:S(2)}, u32[]{:S(2)}) collective-permute-start(f32[4,128,64]{2,1,0:T(8,128)S(1)} %broadcast_add_fusion), channel_id=1, source_target_pairs={{0,32},{32,64},{64,96},{96,128},{128,160},{160,192},{192,224},{1,3... | collective-permute-start | bytes 393224 | tf_op jit(solution)/shard_map/ppermute | solution.py:15
  385.5 7.7 %collective-permute-start.1 = (f32[4,128,64]{2,1,0:T(8,128)S(1)}, f32[4,128,64]{2,1,0:T(8,128)S(1)}, u32[]{:S(2)}, u32[]{:S(2)}) collective-permute-start(f32[4,128,64]{2,1,0:T(8,128)S(1)} %multiply_add_fusion.5), channel_id=1, source_target_pairs={{0,32},{32,64},{64,96},{96,128},{128,160},{160,192},{192,224},{1,3... | collective-permute-start | bytes 393224 | tf_op jit(solution)/shard_map/ppermute | solution.py:15
  393.3 7.7 %collective-permute-start.2 = (f32[4,128,64]{2,1,0:T(8,128)S(1)}, f32[4,128,64]{2,1,0:T(8,128)S(1)}, u32[]{:S(2)}, u32[]{:S(2)}) collective-permute-start(f32[4,128,64]{2,1,0:T(8,128)S(1)} %multiply_add_fusion.4), channel_id=1, source_target_pairs={{0,32},{32,64},{64,96},{96,128},{128,160},{160,192},{192,224},{1,3... | collective-permute-start | bytes 393224 | tf_op jit(solution)/shard_map/ppermute | solution.py:15
  401.1 7.7 %collective-permute-start.3 = (f32[4,128,64]{2,1,0:T(8,128)S(1)}, f32[4,128,64]{2,1,0:T(8,128)S(1)}, u32[]{:S(2)}, u32[]{:S(2)}) collective-permute-start(f32[4,128,64]{2,1,0:T(8,128)S(1)} %multiply_add_fusion.3), channel_id=1, source_target_pairs={{0,32},{32,64},{64,96},{96,128},{128,160},{160,192},{192,224},{1,3... | collective-permute-start | bytes 393224 | tf_op jit(solution)/shard_map/ppermute | solution.py:15
  408.9 7.7 %collective-permute-start.4 = (f32[4,128,64]{2,1,0:T(8,128)S(1)}, f32[4,128,64]{2,1,0:T(8,128)S(1)}, u32[]{:S(2)}, u32[]{:S(2)}) collective-permute-start(f32[4,128,64]{2,1,0:T(8,128)S(1)} %multiply_add_fusion.2), channel_id=1, source_target_pairs={{0,32},{32,64},{64,96},{96,128},{128,160},{160,192},{192,224},{1,3... | collective-permute-start | bytes 393224 | tf_op jit(solution)/shard_map/ppermute | solution.py:15
  416.7 7.7 %collective-permute-start.5 = (f32[4,128,64]{2,1,0:T(8,128)S(1)}, f32[4,128,64]{2,1,0:T(8,128)S(1)}, u32[]{:S(2)}, u32[]{:S(2)}) collective-permute-start(f32[4,128,64]{2,1,0:T(8,128)S(1)} %multiply_add_fusion.1), channel_id=1, source_target_pairs={{0,32},{32,64},{64,96},{96,128},{128,160},{160,192},{192,224},{1,3... | collective-permute-start | bytes 393224 | tf_op jit(solution)/shard_map/ppermute | solution.py:15
  424.5 7.7 %collective-permute-start.6 = (f32[4,128,64]{2,1,0:T(8,128)S(1)}, f32[4,128,64]{2,1,0:T(8,128)S(1)}, u32[]{:S(2)}, u32[]{:S(2)}) collective-permute-start(f32[4,128,64]{2,1,0:T(8,128)S(1)} %multiply_add_fusion), channel_id=1, source_target_pairs={{0,32},{32,64},{64,96},{96,128},{128,160},{160,192},{192,224},{1,3... | collective-permute-start | bytes 393224 | tf_op jit(solution)/shard_map/ppermute | solution.py:15
Sparse Core Ops, SparseCore 0:
  9.9 105.6 all-gather.2
  118.2 90.5 all-gather.4
where the time goes:
time: 614 us; the launch traced here: 611 us
  waiting for transfers between devices  215 us (35%)
  blocking collectives  123 us (20%)
  local copies, waits for them, and re-layouts  82.6 us (13%)
  other arithmetic  75.7 us (12%)
  matrix products  62.4 us (10%)
  starting transfers between devices  30.5 us (5%)
  between operations  13.7 us (2%)
  loops' own time  7.91 us (1%)
    all_to_all x1, blocking collectives, on_device(): lax.all_to_all(result, 'head', split_axis=0, concat_axis=1, tiled=True)  123 us
    all_gather x1, waiting for transfers between devices, on_device(): lax.all_gather(b_panel, 'head', axis=0, tiled=True)  93.1 us
    all_gather x1, waiting for transfers between devices, on_device(): lax.all_gather(c_panel, 'head', axis=0, tiled=True)  75.6 us
    add x40, other arithmetic, advance(): factor[:, None, None] * state_now + update  41.8 us
    ppermute x7, waiting for transfers between devices, passed_along(): return lax.ppermute(block, axis, route)  39.9 us
    all_to_all x3, local copies, waits for them, and re-layouts, on_device(): lax.all_to_all(result, 'head', split_axis=0, concat_axis=1, tiled=True)  34.1 us
    dynamic_update_slice x40, other arithmetic, on_device(): lax.scan(advance, start_state, (jnp.transpose(span_decay), jnp.moveaxis(s...  29.2 us
    dot_general x4, matrix products, head_terms(): jnp.einsum('kts,ksp->ktp', weights, tokens_head, preferred_element_type=j...  27.3 us
  transfers between devices with their start and end apart: 11, of which 10 were waited for; matrix products, arithmetic and copies ran while one was open for 3% of the time, Pallas kernels for 0%

commit v1 on v0

--- a/solution.py
+++ b/solution.py
@@ -40,7 +40,9 @@
         lax.all_to_all(dt_raw, "head", split_axis=1, concat_axis=0, tiled=True),
     )
     b_whole, c_whole = (
-        lax.all_gather(b_panel, "head", axis=0, tiled=True),
+        jnp.concatenate(
+            lax.all_to_all(jnp.stack([b_panel] * lax.axis_size("head")), "head", 0, 0), axis=0
+        ),
         lax.all_gather(c_panel, "head", axis=0, tiled=True),
     )
     length = tokens.shape[0]

time: 614 us -> 636 us (1.036)
  blocking collectives: 123 us -> 144 us
  starting transfers between devices: 30.5 us -> 22.7 us
    all_gather x1 -> x0, waiting for transfers between devices: 93.1 us -> none  [on_device(): lax.all_gather(b_panel, 'head', axis=0, tiled=True)]
    all_to_all x1, waiting for transfers between devices: 4.72 us -> 56.9 us  [on_device(): lax.all_to_all(jnp.stack([b_panel] * lax.axis_size('head')), 'head', 0, 0)]
    all_gather x1, waiting for transfers between devices: 75.6 us -> 123 us  [on_device(): lax.all_gather(c_panel, 'head', axis=0, tiled=True)]
    all_to_all x0 -> x1, blocking collectives: none -> 21.4 us  [on_device(): lax.all_to_all(dt_raw, 'head', split_axis=1, concat_axis=0, tiled=True)]
    all_to_all x1, starting transfers between devices: 11.5 us -> 4.06 us  [on_device(): lax.all_to_all(jnp.stack([b_panel] * lax.axis_size('head')), 'head', 0, 0)]
  transfers between devices with their start and end apart: 11 -> 10, of which waited for: 10 -> 9; matrix products, arithmetic and copies ran while one was open for 3% -> 3% of each run, Pallas kernels for 0% -> 0%
where the time goes in v1:
time: 636 us; the launch traced here: 633 us
  waiting for transfers between devices  221 us (35%)
  blocking collectives  144 us (23%)
  local copies, waits for them, and re-layouts  85.1 us (13%)
  other arithmetic  75.7 us (12%)
  matrix products  61.8 us (10%)
  starting transfers between devices  22.7 us (4%)
  between operations  13.7 us (2%)
  loops' own time  9.32 us (1%)
    all_gather x1, waiting for transfers between devices, on_device(): lax.all_gather(c_panel, 'head', axis=0, tiled=True)  123 us
    all_to_all x1, blocking collectives, on_device(): lax.all_to_all(result, 'head', split_axis=0, concat_axis=1, tiled=True)  122 us
    all_to_all x1, waiting for transfers between devices, on_device(): lax.all_to_all(jnp.stack([b_panel] * lax.axis_size('head')), 'head', 0, 0)  56.9 us
    add x40, other arithmetic, advance(): factor[:, None, None] * state_now + update  41.8 us
    ppermute x7, waiting for transfers between devices, passed_along(): return lax.ppermute(block, axis, route)  39.9 us
    all_to_all x3, local copies, waits for them, and re-layouts, on_device(): lax.all_to_all(result, 'head', split_axis=0, concat_axis=1, tiled=True)  34.1 us
    dynamic_update_slice x40, other arithmetic, on_device(): lax.scan(advance, start_state, (jnp.transpose(span_decay), jnp.moveaxis(s...  29.3 us
    dot_general x4, matrix products, head_terms(): jnp.einsum('kts,ksp->ktp', weights, tokens_head, preferred_element_type=j...  27.5 us
  transfers between devices with their start and end apart: 10, of which 9 were waited for; matrix products, arithmetic and copies ran while one was open for 3% of the time, Pallas kernels for 0%

profile of v1, /device:TPU:2, one launch (start us, length us, event | category | flops | bytes accessed | tf_op | source)
XLA Modules:
  0.0 632.9 jit_solution(10009435555059900436)
XLA Ops:
  7.6 21.4 %all_to_all.53 = bf16[320,32,4]{0,2,1:T(4,128)(2,1)S(1)} all-to-all(bf16[320,32,4]{0,2,1:T(4,128)(2,1)S(1)} %all_to_all.39), channel_id=1, replica_groups=mesh['seq'=8,'head'=32] {'head'}, dimensions={1} | all-to-all | bytes 163840 | tf_op jit(solution)/shard_map/all_to_all | solution.py:40
  29.0 3.0 stack.2
  32.0 4.1 all-to-all-start.1
  36.0 5.4 copy.114
  41.5 56.9 %all-to-all-done.1 = bf16[32,320,128]{2,1,0:T(8,128)(2,1)S(1)} async-done(((bf16[32,320,128]{2,1,0:T(8,128)(2,1)}), bf16[32,320,128]{2,1,0:T(8,128)(2,1)S(1)}, u32[]{:S(2)}, u32[]{:S(2)}) %all-to-all-start.1) | async-done | bytes 2621472 | tf_op jit(solution)/shard_map/all_to_all | solution.py:44
  98.3 5.0 all-to-all-start.2
  104.7 2.4 reduce-window.6
  107.4 123.4 %all-gather.2.cloned.1.call-done = bf16[10240,128]{1,0:T(8,128)(2,1)} async-done(((bf16[320,128]{1,0:T(8,128)(2,1)}), bf16[10240,128]{1,0:T(8,128)(2,1)}) %all-gather.2.cloned.1.call-update) | async-done | bytes 2621456 | tf_op jit(solution)/shard_map/all_gather | solution.py:46
  230.8 7.1 %fusion.19 = f32[40,256,256]{2,1,0:T(8,128)} fusion(bf16[40,256,128]{2,1,0:T(8,128)(2,1)} %bitcast.110, bf16[40,256,128]{2,1,0:T(8,128)(2,1)S(1)} %bitcast.108), kind=kOutput, calls=%fused_computation.52 | convolution fusion | flops 671088640 | bytes 15728640 | tf_op jit(solution)/shard_map/ktn,ksn->kts/dot_general | solution.py:60
  237.9 8.7 %copy.81 = bf16[32,320,256]{1,0,2:T(8,128)(2,1)} copy(bf16[32,320,256]{2,1,0:T(8,128)(2,1)} %bitcast.12) | data formatting | bytes 10485760 | tf_op jit(solution)/shard_map/all_to_all | solution.py:39
  246.6 13.0 %reshape.96 = bf16[40,256,4,64]{1,0,3,2:T(8,128)(2,1)} reshape(bf16[32,320,256]{1,0,2:T(8,128)(2,1)} %copy.81) | data formatting | bytes 10485760 | tf_op jit(solution)/shard_map/reshape | solution.py:61
  259.6 58.3 %while.31 = (s32[]{:T(128)}, f32[4,40,256,64]{2,3,0,1:T(8,128)}, f32[4,40,128,64]{2,3,1,0:T(8,128)}, f32[4,40]{1,0:T(4,128)S(1)}, s32[4]{0:T(128)S(1)}, /*index=...) while((s32[]{:T(128)}, f32[4,40,256,64]{2,3,0,1:T(8,128)}, ...), condition=%wide.region_3.4_spmd, body=%wide.region_2.3_spmd.sunk | while | flops 520441856 | bytes 22825084 | solution.py:69
  262.6 1.4 constant_dynamic-slice_fusion.3
  264.1 6.9 %bitcast_dynamic-update-slice_fusion.4 = f32[4,40,256,64]{2,3,0,1:T(8,128)} fusion(f32[4,40,256,64]{2,3,0,1:T(8,128)} %get-tuple-element.365, s32[]{:T(128)} %get-tuple-element.364, f32[40,256,256]{2,1,0:T(8,128)} %get-tuple-element.383, f32[40,256]{1,0:T(8,128)S(1)} %get-tuple-element.338, f32[40,256]{1,0:T(8,128)S(1)} %dynamic-slice_bitcast_fusion.3, ...), kind=kOutput, calls=%fused_computation.12.clone.1 | convolution fusion | flops 348651520 | bytes 14606848 | tf_op jit(solution)/shard_map/while/body/eval_jaxpr/kts,ksp->ktp/dot_general | solution.py:24
  271.0 3.2 fusion.26
  277.3 1.4 constant_dynamic-slice_fusion.3
  278.7 6.9 %bitcast_dynamic-update-slice_fusion.4 = f32[4,40,256,64]{2,3,0,1:T(8,128)} fusion(f32[4,40,256,64]{2,3,0,1:T(8,128)} %get-tuple-element.365, s32[]{:T(128)} %get-tuple-element.364, f32[40,256,256]{2,1,0:T(8,128)} %get-tuple-element.383, f32[40,256]{1,0:T(8,128)S(1)} %get-tuple-element.338, f32[40,256]{1,0:T(8,128)S(1)} %dynamic-slice_bitcast_fusion.3, ...), kind=kOutput, calls=%fused_computation.12.clone.1 | convolution fusion | flops 348651520 | bytes 14606848 | tf_op jit(solution)/shard_map/while/body/eval_jaxpr/kts,ksp->ktp/dot_general | solution.py:24
  285.6 3.2 fusion.26
  291.8 1.4 constant_dynamic-slice_fusion.3
  293.3 6.8 %bitcast_dynamic-update-slice_fusion.4 = f32[4,40,256,64]{2,3,0,1:T(8,128)} fusion(f32[4,40,256,64]{2,3,0,1:T(8,128)} %get-tuple-element.365, s32[]{:T(128)} %get-tuple-element.364, f32[40,256,256]{2,1,0:T(8,128)} %get-tuple-element.383, f32[40,256]{1,0:T(8,128)S(1)} %get-tuple-element.338, f32[40,256]{1,0:T(8,128)S(1)} %dynamic-slice_bitcast_fusion.3, ...), kind=kOutput, calls=%fused_computation.12.clone.1 | convolution fusion | flops 348651520 | bytes 14606848 | tf_op jit(solution)/shard_map/while/body/eval_jaxpr/kts,ksp->ktp/dot_general | solution.py:24
  300.1 3.2 fusion.26
  306.4 1.4 constant_dynamic-slice_fusion.3
  307.9 6.9 %bitcast_dynamic-update-slice_fusion.4 = f32[4,40,256,64]{2,3,0,1:T(8,128)} fusion(f32[4,40,256,64]{2,3,0,1:T(8,128)} %get-tuple-element.365, s32[]{:T(128)} %get-tuple-element.364, f32[40,256,256]{2,1,0:T(8,128)} %get-tuple-element.383, f32[40,256]{1,0:T(8,128)S(1)} %get-tuple-element.338, f32[40,256]{1,0:T(8,128)S(1)} %dynamic-slice_bitcast_fusion.3, ...), kind=kOutput, calls=%fused_computation.12.clone.1 | convolution fusion | flops 348651520 | bytes 14606848 | tf_op jit(solution)/shard_map/while/body/eval_jaxpr/kts,ksp->ktp/dot_general | solution.py:24
  314.7 3.2 fusion.26
  317.9 8.5 %copy.85 = f32[4,40,128,64]{3,2,0,1:T(8,128)} copy(f32[4,40,128,64]{2,3,1,0:T(8,128)} %get-tuple-element.101) | data formatting | bytes 10485760 | tf_op jit(solution)/shard_map/while | solution.py:69
  326.5 74.1 %while.32 = (s32[]{:T(128)}, f32[4,128,64]{2,1,0:T(8,128)S(1)}, f32[4]{0:T(128)S(1)}, f32[40,4,128,64]{3,2,1,0:T(8,128)}, f32[40,4]{1,0:T(8,128)S(1)}, /*index=5...) while((s32[]{:T(128)}, f32[4,128,64]{2,1,0:T(8,128)S(1)}, ...), condition=%wide.region_5.6_spmd.clone, body=%wide.region_4.5_spmd.clone.sunk | while | flops 131083 | bytes 787189 | solution.py:83
  327.3 1.2 bitcast_add_fusion.2
  329.3 1.0 bitcast_add_fusion.2
  331.1 1.0 bitcast_add_fusion.2
  334.8 1.0 bitcast_add_fusion.2
  342.2 1.0 bitcast_add_fusion.2
  349.6 1.0 bitcast_add_fusion.2
  351.4 1.0 bitcast_add_fusion.2
  358.8 1.0 bitcast_add_fusion.2
  360.6 1.0 bitcast_add_fusion.2
  368.1 1.0 bitcast_add_fusion.2
  369.9 1.0 bitcast_add_fusion.2
  371.7 1.0 bitcast_add_fusion.2
  377.3 1.0 bitcast_add_fusion.2
  379.1 1.0 bitcast_add_fusion.2
  381.0 1.0 bitcast_add_fusion.2
  382.8 1.0 bitcast_add_fusion.2
  390.3 1.0 bitcast_add_fusion.2
  392.2 1.0 bitcast_add_fusion.2
  395.9 1.0 bitcast_add_fusion.2
  400.8 1.9 collective-permute-start
  402.7 5.8 collective-permute-done
  408.5 1.9 collective-permute-start.1
  410.5 5.8 collective-permute-done.1
  416.3 1.9 collective-permute-start.2
  418.3 5.8 collective-permute-done.2
  424.1 1.9 collective-permute-start.3
  426.0 5.8 collective-permute-done.3
  431.9 1.9 collective-permute-start.4
  433.8 5.8 collective-permute-done.4
  439.7 1.9 collective-permute-start.5
  441.7 5.7 collective-permute-done.5
  447.5 2.1 collective-permute-start.6
  449.8 5.4 collective-permute-done.6
  455.2 14.5 %fusion.12 = bf16[40,256,4,64]{1,3,2,0:T(8,128)(2,1)} fusion(f32[4,40,256,64]{2,3,0,1:T(8,128)} %get-tuple-element.99, bf16[40,256,4,64]{1,0,3,2:T(8,128)(2,1)} %get-tuple-element.418, f32[4]{0:T(128)S(1)} %dynamic_slice.34, f32[40,256,4]{1,2,0:T(4,128)S(1)} %copy.87, bf16[40,256,128,1]{2,1,3,0:T(8,128)(2,1)S(1)} %bitcast.111, ...), kind=kOutput, calls=%fused_computation.28 | convolution fusion | flops 690749440 | bytes 29131408 | tf_op jit(solution)/shard_map/ktn,khnp->kthp/dot_general | solution.py:94
  469.7 15.3 %copy.94 = bf16[40,256,4,64]{3,2,1,0:T(4,128)(2,1)} copy(bf16[40,256,4,64]{1,3,2,0:T(8,128)(2,1)} %fusion.12) | data formatting | bytes 10485760 | tf_op jit(solution)/shard_map/all_to_all | solution.py:102
  485.0 15.7 %reshape.99 = bf16[32,320,256]{2,1,0:T(8,128)(2,1)} reshape(bf16[40,256,4,64]{3,2,1,0:T(4,128)(2,1)} %copy.94) | data formatting | bytes 10485760 | tf_op jit(solution)/shard_map/all_to_all | solution.py:102
  500.7 122.3 %all_to_all.54 = bf16[32,320,256]{2,1,0:T(8,128)(2,1)S(1)} all-to-all(bf16[32,320,256]{2,1,0:T(8,128)(2,1)} %reshape.99), channel_id=1, replica_groups=mesh['seq'=8,'head'=32] {'head'}, dimensions={0} | all-to-all | bytes 10485760 | tf_op jit(solution)/shard_map/all_to_all | solution.py:102
  623.0 3.0 copy.104
  (211 shorter events, 61.0 us)
Async XLA Ops:
  32.0 66.4 %all-to-all-start.1 = ((bf16[32,320,128]{2,1,0:T(8,128)(2,1)}), bf16[32,320,128]{2,1,0:T(8,128)(2,1)S(1)}, u32[]{:S(2)}, u32[]{:S(2)}) async-start(bf16[32,320,128]{2,1,0:T(8,128)(2,1)} %stack.2), calls=%async_computation.1 | async-start | bytes 5242880 | tf_op jit(solution)/shard_map/all_to_all | solution.py:44
  98.3 5.8 copy-start.2
  98.3 5.9 copy-start.3
  98.3 139.6 %all-to-all-start.2 = ((bf16[320,32,256]{2,0,1:T(8,128)(2,1)}), bf16[320,32,256]{2,0,1:T(8,128)(2,1)}, u32[]{:S(2)}, u32[]{:S(2)}) async-start(bf16[320,32,256]{2,0,1:T(8,128)(2,1)} %bitcast.105), calls=%async_computation.2 | async-start | bytes 10485760 | tf_op jit(solution)/shard_map/all_to_all | solution.py:39
  103.4 127.4 %all-gather.2.cloned.1.call-start = ((), (), s32[]{:S(2)}) async-start(), calls=%async_computation.4 | async-start | bytes 2703360 | tf_op jit(solution)/shard_map/all_gather | solution.py:46
  317.9 8.6 %copy-start.1 = (f32[40,4]{1,0:T(8,128)S(1)}, f32[40,4]{1,0:T(8,128)}, u32[]{:S(2)}) copy-start(f32[40,4]{1,0:T(8,128)} %custom-call.6) | copy-start | bytes 1924
  326.5 115.1 %copy-start.4 = (f32[128]{0:T(128)S(1)}, f32[128]{0:T(128)}, u32[]{:S(2)}) copy-start(f32[128]{0:T(128)} %param.17) | copy-start | bytes 1540
  326.5 128.7 %copy-start = (bf16[10240,128]{1,0:T(8,128)(2,1)S(1)}, bf16[10240,128]{1,0:T(8,128)(2,1)}, u32[]{:S(2)}) copy-start(bf16[10240,128]{1,0:T(8,128)(2,1)} %all-gather.2.cloned.1.call-done) | copy-start | bytes 7864324
  400.8 7.7 %collective-permute-start = (f32[4,128,64]{2,1,0:T(8,128)S(1)}, f32[4,128,64]{2,1,0:T(8,128)S(1)}, u32[]{:S(2)}, u32[]{:S(2)}) collective-permute-start(f32[4,128,64]{2,1,0:T(8,128)S(1)} %broadcast_add_fusion), channel_id=1, source_target_pairs={{0,32},{32,64},{64,96},{96,128},{128,160},{160,192},{192,224},{1,3... | collective-permute-start | bytes 393224 | tf_op jit(solution)/shard_map/ppermute | solution.py:15
  408.5 7.7 %collective-permute-start.1 = (f32[4,128,64]{2,1,0:T(8,128)S(1)}, f32[4,128,64]{2,1,0:T(8,128)S(1)}, u32[]{:S(2)}, u32[]{:S(2)}) collective-permute-start(f32[4,128,64]{2,1,0:T(8,128)S(1)} %multiply_add_fusion.5), channel_id=1, source_target_pairs={{0,32},{32,64},{64,96},{96,128},{128,160},{160,192},{192,224},{1,3... | collective-permute-start | bytes 393224 | tf_op jit(solution)/shard_map/ppermute | solution.py:15
  416.3 7.7 %collective-permute-start.2 = (f32[4,128,64]{2,1,0:T(8,128)S(1)}, f32[4,128,64]{2,1,0:T(8,128)S(1)}, u32[]{:S(2)}, u32[]{:S(2)}) collective-permute-start(f32[4,128,64]{2,1,0:T(8,128)S(1)} %multiply_add_fusion.4), channel_id=1, source_target_pairs={{0,32},{32,64},{64,96},{96,128},{128,160},{160,192},{192,224},{1,3... | collective-permute-start | bytes 393224 | tf_op jit(solution)/shard_map/ppermute | solution.py:15
  424.1 7.7 %collective-permute-start.3 = (f32[4,128,64]{2,1,0:T(8,128)S(1)}, f32[4,128,64]{2,1,0:T(8,128)S(1)}, u32[]{:S(2)}, u32[]{:S(2)}) collective-permute-start(f32[4,128,64]{2,1,0:T(8,128)S(1)} %multiply_add_fusion.3), channel_id=1, source_target_pairs={{0,32},{32,64},{64,96},{96,128},{128,160},{160,192},{192,224},{1,3... | collective-permute-start | bytes 393224 | tf_op jit(solution)/shard_map/ppermute | solution.py:15
  431.9 7.7 %collective-permute-start.4 = (f32[4,128,64]{2,1,0:T(8,128)S(1)}, f32[4,128,64]{2,1,0:T(8,128)S(1)}, u32[]{:S(2)}, u32[]{:S(2)}) collective-permute-start(f32[4,128,64]{2,1,0:T(8,128)S(1)} %multiply_add_fusion.2), channel_id=1, source_target_pairs={{0,32},{32,64},{64,96},{96,128},{128,160},{160,192},{192,224},{1,3... | collective-permute-start | bytes 393224 | tf_op jit(solution)/shard_map/ppermute | solution.py:15
  439.7 7.7 %collective-permute-start.5 = (f32[4,128,64]{2,1,0:T(8,128)S(1)}, f32[4,128,64]{2,1,0:T(8,128)S(1)}, u32[]{:S(2)}, u32[]{:S(2)}) collective-permute-start(f32[4,128,64]{2,1,0:T(8,128)S(1)} %multiply_add_fusion.1), channel_id=1, source_target_pairs={{0,32},{32,64},{64,96},{96,128},{128,160},{160,192},{192,224},{1,3... | collective-permute-start | bytes 393224 | tf_op jit(solution)/shard_map/ppermute | solution.py:15
  447.5 7.7 %collective-permute-start.6 = (f32[4,128,64]{2,1,0:T(8,128)S(1)}, f32[4,128,64]{2,1,0:T(8,128)S(1)}, u32[]{:S(2)}, u32[]{:S(2)}) collective-permute-start(f32[4,128,64]{2,1,0:T(8,128)S(1)} %multiply_add_fusion), channel_id=1, source_target_pairs={{0,32},{32,64},{64,96},{96,128},{128,160},{160,192},{192,224},{1,3... | collective-permute-start | bytes 393224 | tf_op jit(solution)/shard_map/ppermute | solution.py:15
Sparse Core Ops, SparseCore 0:
  106.8 123.9 all-gather.1
